TPU v7x, 512 devices: a whole 4x8x8 slice. The times are simulated.
512 devices in a mesh: patch: 64 (over z, y), grp: 8 (over x, core).
Axes of the slice: x: 4, y: 8, z: 8, core: 2. Of those that a mesh axis runs over, the one named last changes fastest.
Arguments:
- right_side: bfloat16 [16, 8192, 128], P('grp', 'patch'), may hold values from -6 to 6
- coefficient: bfloat16 [16, 8192, 128], P('grp', 'patch'), may hold values from 0.19921875 to 5
- row_counts: int32 [64], P('patch'), may hold values from 1 to 2, 80 in all
Outputs:
- solution: float32 [16, 8192, 128], P('grp', 'patch')
Inputs may be any that keep to these rules, and one draw needn't show every extreme that they name: `row_counts`: each index of patch holds 1 to 2 rows, the same in every slab, 80 in all, and some index holds exactly 2.
All inputs are finite; a program needn't handle non-finite values. No bound on the sum of `row_counts` on one device may be relied on, other than what follows from the above.
Results may differ from a plain program's by a relative error of at most 0.0003.
Values sent between devices are 32-bit elements; how exact they have to be, the bound alone decides.
A program may use at most 64 MiB of HBM per device.

v0:
```python
import jax
import jax.numpy as jnp
from jax import lax
from jax.sharding import PartitionSpec as P

CAP = 2
CYCLES = 2
PRE = 2
COARSE_ITERS = 4


relax_factor = 0.8


def shifted_2(value, axis, steps):
    count = lax.axis_size(axis)
    initial, last = (max(0, -steps), min(count, count - steps))
    return lax.ppermute(value, axis, [(source, source + steps) for source in range(initial, last)])


def padded_2(block, sides, width):
    for axis, dim in sides:
        count = lax.axis_size(axis)
        forward = [(i, i + 1) for i in range(count - 1)]
        backward = [(target, source) for source, target in forward]
        low = lax.ppermute(
            lax.slice_in_dim(block, block.shape[dim] - width, None, axis=dim), axis, forward
        )
        high = lax.ppermute(lax.slice_in_dim(block, 0, width, axis=dim), axis, backward)
        block = jnp.concatenate([low, block, high], axis=dim)
    return block


def shifted(padded, axis_number, offset):
    spans = [slice(1, -1), slice(1, -1), slice(1, -1)]
    spans[axis_number] = slice(1 + offset, padded.shape[axis_number] - 1 + offset)
    return padded[tuple(spans)]


def apply_operator(padded_field, padded_coeff):
    center_field = shifted(padded_field, 0, 0)
    center_coeff = shifted(padded_coeff, 0, 0)
    result = jnp.zeros_like(center_field)
    for axis_number in range(3):
        for offset in (-1, 1):
            weight = 0.5 * (center_coeff + shifted(padded_coeff, axis_number, offset))
            result = result + weight * (center_field - shifted(padded_field, axis_number, offset))
    return result


def diagonal_of(padded_coeff):
    center_coeff = shifted(padded_coeff, 0, 0)
    result = jnp.zeros_like(center_coeff)
    for axis_number in range(3):
        for offset in (-1, 1):
            result = result + 0.5 * (center_coeff + shifted(padded_coeff, axis_number, offset))
    return result


def restrict(field):
    whole_x, whole_y, whole_z = field.shape
    blocks = field.reshape(whole_x // 2, 2, whole_y // 2, 2, whole_z // 2, 2)
    return 0.5 * jnp.sum(blocks, axis=(1, 3, 5))


def prolong(field):
    return jnp.repeat(jnp.repeat(jnp.repeat(field, 2, axis=0), 2, axis=1), 2, axis=2)


def neighbour_pad(field, valid_rows):
    whole_x, whole_y, whole_z = field.shape
    last_plane = lax.dynamic_slice_in_dim(field, valid_rows - 1, 1, 1)
    from_below = shifted_2(last_plane, "patch", 1)
    from_above = shifted_2(field[:, :1, :], "patch", -1)
    extended = padded_2(field, (("grp", 0),), 1)
    low_face = extended[:1]
    high_face = extended[-1:]
    zero_plane = jnp.zeros((whole_x, 1, whole_z), field.dtype)
    middle = jnp.concatenate([from_below, field, zero_plane], axis=1)
    middle = lax.dynamic_update_slice_in_dim(middle, from_above, valid_rows + 1, 1)
    edge_rows = jnp.zeros((1, 1, whole_z), field.dtype)
    low_face = jnp.concatenate([edge_rows, low_face, edge_rows], axis=1)
    high_face = jnp.concatenate([edge_rows, high_face, edge_rows], axis=1)
    stacked = jnp.concatenate([low_face, middle, high_face], axis=0)
    return jnp.pad(stacked, ((0, 0), (0, 0), (1, 1)))


def coarse_total(value):
    return lax.psum(value, ("patch", "grp"))


def coarse_solve(coarse_rhs, coarse_padded, coarse_valid, coarse_mask):
    estimate = jnp.zeros_like(coarse_rhs)
    remain = coarse_rhs
    search = coarse_rhs
    norm_now = coarse_total(jnp.sum(remain * remain))
    for iteration in range(COARSE_ITERS):
        mapped = apply_operator(neighbour_pad(search, coarse_valid), coarse_padded) * coarse_mask
        step_size = norm_now / coarse_total(jnp.sum(search * mapped))
        estimate = estimate + step_size * search
        remain = remain - step_size * mapped
        norm_next = coarse_total(jnp.sum(remain * remain))
        search = remain + norm_next / norm_now * search
        norm_now = norm_next
    return estimate


def relax(solution, source, padded_coeff, fine_diagonal, fine_valid, fine_mask):
    mapped = apply_operator(neighbour_pad(solution, fine_valid), padded_coeff)
    return (solution + relax_factor * (source - mapped) / fine_diagonal) * fine_mask


def per_device(right_side, coefficient, row_counts):
    slab_x, padded_y, depth_z = right_side.shape
    patch_rows = row_counts[0]
    patch_edge = padded_y // CAP
    fine_valid = patch_rows * patch_edge
    coarse_valid = patch_rows * (patch_edge // 2)
    fine_mask = (lax.broadcasted_iota(jnp.int32, (1, padded_y, 1), 1) < fine_valid).astype(
        jnp.float32
    )
    source = right_side.astype(jnp.float32) * fine_mask
    conduct = coefficient.astype(jnp.float32) * fine_mask
    padded_coeff = neighbour_pad(conduct, fine_valid)
    fine_diagonal = jnp.where(fine_mask > 0, diagonal_of(padded_coeff), 1.0)
    local_coarse = 0.25 * restrict(conduct)
    coarse_mask = (lax.broadcasted_iota(jnp.int32, (1, padded_y // 2, 1), 1) < coarse_valid).astype(
        jnp.float32
    )
    coarse_padded = neighbour_pad(local_coarse, coarse_valid)
    solution = jnp.zeros_like(source)
    for cycle_index in range(CYCLES):
        for sweep_index in range(PRE):
            solution = relax(solution, source, padded_coeff, fine_diagonal, fine_valid, fine_mask)
        mapped = apply_operator(neighbour_pad(solution, fine_valid), padded_coeff)
        residual = (source - mapped) * fine_mask
        coarse_rhs = restrict(residual)
        correction = coarse_solve(coarse_rhs, coarse_padded, coarse_valid, coarse_mask)
        solution = solution + prolong(correction) * fine_mask
        solution = relax(solution, source, padded_coeff, fine_diagonal, fine_valid, fine_mask)
    return solution


def solution(mesh):
    in_specs = (P("grp", "patch", None), P("grp", "patch", None), P("patch"))
    out_specs = P("grp", "patch", None)
    return jax.shard_map(
        per_device, mesh=mesh, in_specs=in_specs, out_specs=out_specs, check_vma=False
    )
```

profile of v0, /device:TPU:1, one launch (start us, length us, event | category | flops | bytes accessed | tf_op | source)
XLA Modules:
  0.0 1677.5 jit_solution(4072590902660409576)
XLA Ops:
  1.3 4.7 collective-permute-start.3
  6.0 8.7 collective-permute-start.7
  17.6 4.0 collective-permute-start
  21.6 5.5 reduce_sum.197
  38.5 3.6 collective-permute-start.18
  53.9 4.3 collective-permute-start.12
  65.2 4.6 collective-permute-start.16
  70.1 5.5 reduce_sum.193
  84.5 4.3 collective-permute-start.21
  94.0 111.7 %all-reduce.19 = (f32[]{:T(128)}, f32[]{:T(128)}) all-reduce(f32[]{:T(128)} %get-tuple-element.87, f32[]{:T(128)} %get-tuple-element.23), channel_id=1, replica_groups=mesh['patch'=64,'grp'=8] {'patch','grp'}, use_global_device_ids=true, to_apply=%region_3.4 | all-reduce | flops 2 | bytes 16 | tf_op jit(solution)/shard_map/psum | solution.py:89
  207.7 95.0 %psum.114 = f32[]{:T(128)} all-reduce(f32[]{:T(128)} %multiply_reduce_fusion.11), channel_id=1, replica_groups=mesh['patch'=64,'grp'=8] {'patch','grp'}, use_global_device_ids=true, to_apply=%region_9.10 | all-reduce | flops 1 | bytes 8 | tf_op jit(solution)/shard_map/psum | solution.py:89
  317.2 99.0 %psum.115 = f32[]{:T(128)} all-reduce(f32[]{:T(128)} %get-tuple-element.21), channel_id=1, replica_groups=mesh['patch'=64,'grp'=8] {'patch','grp'}, use_global_device_ids=true, to_apply=%region_11.12 | all-reduce | flops 1 | bytes 8 | tf_op jit(solution)/shard_map/psum | solution.py:89
  418.2 95.3 %psum.116 = f32[]{:T(128)} all-reduce(f32[]{:T(128)} %get-tuple-element.19), channel_id=1, replica_groups=mesh['patch'=64,'grp'=8] {'patch','grp'}, use_global_device_ids=true, to_apply=%region_13.14 | all-reduce | flops 1 | bytes 8 | tf_op jit(solution)/shard_map/psum | solution.py:89
  527.6 99.3 %psum.117 = f32[]{:T(128)} all-reduce(f32[]{:T(128)} %get-tuple-element.17), channel_id=1, replica_groups=mesh['patch'=64,'grp'=8] {'patch','grp'}, use_global_device_ids=true, to_apply=%region_15.16 | all-reduce | flops 1 | bytes 8 | tf_op jit(solution)/shard_map/psum | solution.py:89
  628.8 95.6 %psum.118 = f32[]{:T(128)} all-reduce(f32[]{:T(128)} %multiply_reduce_fusion.7), channel_id=1, replica_groups=mesh['patch'=64,'grp'=8] {'patch','grp'}, use_global_device_ids=true, to_apply=%region_17.18 | all-reduce | flops 1 | bytes 8 | tf_op jit(solution)/shard_map/psum | solution.py:89
  737.8 99.7 %psum.119 = f32[]{:T(128)} all-reduce(f32[]{:T(128)} %fusion.322), channel_id=1, replica_groups=mesh['patch'=64,'grp'=8] {'patch','grp'}, use_global_device_ids=true, to_apply=%region_19.20 | all-reduce | flops 1 | bytes 8 | tf_op jit(solution)/shard_map/psum | solution.py:89
  841.9 4.4 collective-permute-start.38
  852.1 4.3 collective-permute-start.40
  865.7 4.3 collective-permute-start.44
  879.3 4.3 collective-permute-start.48
  892.8 5.5 reduce_sum.207
  901.8 4.3 collective-permute-start.52
  908.0 3.6 collective-permute-start.54
  913.0 3.8 collective-permute-done.53
  917.6 113.6 %all-reduce.18 = (f32[]{:T(128)}, f32[]{:T(128)}) all-reduce(f32[]{:T(128)} %get-tuple-element.78, f32[]{:T(128)} %get-tuple-element.15), channel_id=1, replica_groups=mesh['patch'=64,'grp'=8] {'patch','grp'}, use_global_device_ids=true, to_apply=%region_23.24 | all-reduce | flops 2 | bytes 16 | tf_op jit(solution)/shard_map/psum | solution.py:89
  1033.1 95.3 %psum.122 = f32[]{:T(128)} all-reduce(f32[]{:T(128)} %multiply_reduce_fusion.4), channel_id=1, replica_groups=mesh['patch'=64,'grp'=8] {'patch','grp'}, use_global_device_ids=true, to_apply=%region_27.28 | all-reduce | flops 1 | bytes 8 | tf_op jit(solution)/shard_map/psum | solution.py:89
  1141.7 99.3 %psum.123 = f32[]{:T(128)} all-reduce(f32[]{:T(128)} %get-tuple-element.13), channel_id=1, replica_groups=mesh['patch'=64,'grp'=8] {'patch','grp'}, use_global_device_ids=true, to_apply=%region_29.30 | all-reduce | flops 1 | bytes 8 | tf_op jit(solution)/shard_map/psum | solution.py:89
  1243.1 95.3 %psum.124 = f32[]{:T(128)} all-reduce(f32[]{:T(128)} %get-tuple-element.11), channel_id=1, replica_groups=mesh['patch'=64,'grp'=8] {'patch','grp'}, use_global_device_ids=true, to_apply=%region_31.32 | all-reduce | flops 1 | bytes 8 | tf_op jit(solution)/shard_map/psum | solution.py:89
  1351.8 99.8 %psum.125 = f32[]{:T(128)} all-reduce(f32[]{:T(128)} %get-tuple-element.9), channel_id=1, replica_groups=mesh['patch'=64,'grp'=8] {'patch','grp'}, use_global_device_ids=true, to_apply=%region_33.34 | all-reduce | flops 1 | bytes 8 | tf_op jit(solution)/shard_map/psum | solution.py:89
  1453.6 95.5 %psum.126 = f32[]{:T(128)} all-reduce(f32[]{:T(128)} %multiply_reduce_fusion), channel_id=1, replica_groups=mesh['patch'=64,'grp'=8] {'patch','grp'}, use_global_device_ids=true, to_apply=%region_35.36 | all-reduce | flops 1 | bytes 8 | tf_op jit(solution)/shard_map/psum | solution.py:89
  1562.5 99.8 %psum.127 = f32[]{:T(128)} all-reduce(f32[]{:T(128)} %fusion.321), channel_id=1, replica_groups=mesh['patch'=64,'grp'=8] {'patch','grp'}, use_global_device_ids=true, to_apply=%region_37.38 | all-reduce | flops 1 | bytes 8 | tf_op jit(solution)/shard_map/psum | solution.py:89
  1666.7 4.4 collective-permute-start.70
  (265 shorter events, 178.1 us)
Async XLA Ops:
  0.0 36.5 %collective-permute-start.4 = (f32[2,1,128]{2,1,0:T(1,128)S(1)}, f32[2,1,128]{2,1,0:T(1,128)S(1)}, u32[]{:S(2)}, u32[]{:S(2)}) collective-permute-start(f32[2,1,128]{2,1,0:T(1,128)S(1)} %broadcast.174), channel_id=1, source_target_pairs={{8,0},{16,8},{24,16},{32,24},{40,32},{48,40},{56,48},{64,56},{72,6... | collective-permute-start | bytes 3080 | tf_op jit(solution)/shard_map/ppermute | solution.py:18
  1.3 28.8 %collective-permute-start.3 = (f32[2,1,128]{2,1,0:T(1,128)S(1)}, f32[2,1,128]{2,1,0:T(1,128)S(1)}, u32[]{:S(2)}, u32[]{:S(2)}) collective-permute-start(f32[2,1,128]{2,1,0:T(1,128)S(1)} %broadcast.174), channel_id=1, source_target_pairs={{0,8},{8,16},{16,24},{24,32},{32,40},{40,48},{48,56},{56,64},{64,7... | collective-permute-start | bytes 3080 | tf_op jit(solution)/shard_map/ppermute | solution.py:18
  6.0 32.5 %collective-permute-start.7 = (f32[1,128,128]{2,1,0:T(8,128)S(1)}, f32[1,128,128]{2,1,0:T(8,128)S(1)}, u32[]{:S(2)}, u32[]{:S(2)}) collective-permute-start(f32[1,128,128]{2,1,0:T(8,128)S(1)} %broadcast.177), channel_id=1, source_target_pairs={{1,0},{2,1},{3,2},{4,3},{5,4},{6,5},{7,6},{9,8},{10,9},{11,10},{12... | collective-permute-start | bytes 196616 | tf_op jit(solution)/shard_map/ppermute | solution.py:29
  16.3 15.8 collective-permute-start.1
  17.6 16.4 collective-permute-start
  30.1 12.0 collective-permute-start.5
  32.1 10.1 collective-permute-start.2
  36.6 56.6 %collective-permute-start.22 = (f32[1,64,64]{2,1,0:T(8,128)S(1)}, f32[1,64,64]{2,1,0:T(8,128)S(1)}, u32[]{:S(2)}, u32[]{:S(2)}) collective-permute-start(f32[1,64,64]{2,1,0:T(8,128)S(1)} %get-tuple-element.91), channel_id=1, source_target_pairs={{1,0},{2,1},{3,2},{4,3},{5,4},{6,5},{7,6},{9,8},{10,9},{11,10},{12... | collective-permute-start | bytes 49160 | tf_op jit(solution)/shard_map/ppermute | solution.py:29
  38.5 54.6 %collective-permute-start.18 = (f32[1,64,64]{2,1,0:T(8,128)S(1)}, f32[1,64,64]{2,1,0:T(8,128)S(1)}, u32[]{:S(2)}, u32[]{:S(2)}) collective-permute-start(f32[1,64,64]{2,1,0:T(8,128)S(1)} %get-tuple-element.91), channel_id=1, source_target_pairs={{0,1},{1,2},{2,3},{3,4},{4,5},{5,6},{6,7},{8,9},{9,10},{10,11},{11... | collective-permute-start | bytes 49160 | tf_op jit(solution)/shard_map/ppermute | solution.py:26
  61.6 8.2 collective-permute-start.15
  63.9 18.5 %collective-permute-start.17 = (f32[1,1,64]{2,1,0:T(1,128)S(1)}, f32[1,1,64]{2,1,0:T(1,128)S(1)}, u32[]{:S(2)}, u32[]{:S(2)}) collective-permute-start(f32[1,1,64]{2,1,0:T(1,128)S(1)} %slice.888), channel_id=1, source_target_pairs={{8,0},{16,8},{24,16},{32,24},{40,32},{48,40},{56,48},{64,56},{72,6... | collective-permute-start | bytes 776 | tf_op jit(solution)/shard_map/ppermute | solution.py:18
  65.2 19.3 %collective-permute-start.16 = (f32[1,1,64]{2,1,0:T(1,128)S(1)}, f32[1,1,64]{2,1,0:T(1,128)S(1)}, u32[]{:S(2)}, u32[]{:S(2)}) collective-permute-start(f32[1,1,64]{2,1,0:T(1,128)S(1)} %fusion.323), channel_id=1, source_target_pairs={{0,8},{8,16},{16,24},{24,32},{32,40},{40,48},{48,56},{56,64},{64,7... | collective-permute-start | bytes 776 | tf_op jit(solution)/shard_map/ppermute | solution.py:18
  79.0 9.8 collective-permute-start.19
  82.4 10.8 collective-permute-start.23
  84.5 8.6 collective-permute-start.21
  304.1 9.4 collective-permute-start.24
  305.7 10.8 collective-permute-start.27
  514.9 8.9 collective-permute-start.28
  516.9 9.9 collective-permute-start.31
  727.1 9.9 collective-permute-start.35
  839.2 9.0 collective-permute-start.36
  852.1 9.9 collective-permute-start.40
  865.7 9.9 collective-permute-start.44
  879.3 9.9 collective-permute-start.48
  901.8 11.2 collective-permute-start.52
  906.0 10.7 collective-permute-start.55
  908.0 8.8 collective-permute-start.54
  1129.8 8.2 collective-permute-start.56
  1131.1 9.9 collective-permute-start.59
  1341.1 9.9 collective-permute-start.63
  1551.8 9.9 collective-permute-start.67
  1664.0 8.9 collective-permute-start.68
  (41 other events, 258.3 us)
where the time goes:
time: 1680 us
  blocking collectives  1390 us (83%)
  starting transfers between devices  175 us (10%)
  waiting for transfers between devices  45 us (3%)
  other arithmetic  23.8 us (1%)
  between operations  21.1 us (1%)
  local copies, waits for them, and re-layouts  18 us (1%)
    psum x14, blocking collectives, coarse_total(): return lax.psum(value, ('patch', 'grp'))  1390 us
    ppermute x36, starting transfers between devices, shifted_2(): lax.ppermute(value, axis, [(source, source + steps) for source in range(i...  74.4 us
    ppermute x18, starting transfers between devices, padded_2(): lax.ppermute(lax.slice_in_dim(block, block.shape[dim] - width, None, axis...  52.1 us
    ppermute x18, starting transfers between devices, padded_2(): lax.ppermute(lax.slice_in_dim(block, 0, width, axis=dim), axis, backward)  48.9 us
  transfers between devices with their start and end apart: 72, of which 14 were waited for; matrix products, arithmetic and copies ran while one was open for 1% of the time, Pallas kernels for 0%

commit v1 on v0

v1 whole, which is shorter than its diff:
```python
import functools

import jax
import jax.numpy as jnp
from jax import lax
from jax.experimental import pallas as pl
from jax.experimental.pallas import tpu as pltpu
from jax.sharding import PartitionSpec as P

MESH = pl.DeviceIdType.MESH
CYCLES = 2
KRYLOV = 4
PATCH = 64
OWN = 128
HALO = 24
EXT = OWN + 2 * HALO
GUARD = 8
ROWS = EXT + 2 * GUARD
FIRST = GUARD + HALO
WIDE = 10
LANES = 128
TILES = EXT // 8
C_EXT = EXT // 2
C_ROWS = C_EXT + 2 * GUARD
C_TILES = C_EXT // 8
C_SENT = 48
C_SKIP = C_EXT - C_SENT
F32 = jnp.float32


def lane_roll(x, steps):
    return pltpu.roll(x, steps % LANES, axis=1)


def loop(count, body):
    def step(i, carry):
        body(i)
        return carry

    lax.fori_loop(0, count, step, 0)


def at_tile(i, offset):
    return pl.ds(offset + 8 * i, 8)


def kernel(n_patch, n_grp, rs_ref, cf_ref, count_ref, out_ref,
           own, last, low, high, kf, gain, diag, cx, cy, cz, u0, u1, total, coarse, packed, gathered,
           kc, ccx, ccy, ccz, cdiag, basis, part, parts,
           p_send, p_recv, b_send, b_recv, w_send, w_recv, c_send, c_recv, s_send, s_recv):
    half = n_grp // 2
    p = lax.axis_index("patch")
    g = lax.axis_index("grp")
    count = count_ref[0]
    two = count >= 2

    lane = lax.broadcasted_iota(jnp.int32, (8, LANES), 1)
    row = lax.broadcasted_iota(jnp.int32, (8, LANES), 0)
    even = lane % 2 == 0
    zero = jnp.zeros((8, LANES), F32)

    def inside(dp, dg):
        return (p + dp >= 0) & (p + dp < n_patch) & (g + dg >= 0) & (g + dg < n_grp)

    barrier = pltpu.get_barrier_semaphore()
    for dp in (-1, 1):
        for dg in (-2, -1, 1, 2):
            peer = (lax.rem(p + dp + n_patch, n_patch), lax.rem(g + dg + n_grp, n_grp))
            pl.semaphore_signal(barrier, inc=1, device_id=peer, device_id_type=MESH)
    for dg in range(1, n_grp):
        pl.semaphore_signal(barrier, inc=1, device_id=(p, lax.rem(g + dg, n_grp)), device_id_type=MESH)

    def greet(i):
        peer = (lax.rem(p + i + 1, n_patch), g)
        pl.semaphore_signal(barrier, inc=1, device_id=peer, device_id_type=MESH)

    loop(n_patch - 1, greet)

    for a, ref in ((0, cf_ref), (1, rs_ref)):
        for w in range(2):
            def stage(i, a=a, ref=ref, w=w):
                rows = pl.ds(16 * i, 16)
                at = lax.broadcasted_iota(jnp.int32, (16, LANES), 0) + 16 * i
                value = jnp.where(at < PATCH * count, ref[w, rows, :].astype(F32), 0.0)
                own[a, w, rows, :] = value
                kf[a, 4 + w, pl.ds(FIRST + 16 * i, 16), :] = value

            loop(OWN // 16, stage)
            last[a, w] = jnp.where(two, own[a, w, OWN - HALO:, :], own[a, w, PATCH - HALO:PATCH, :])

    guards = jnp.zeros((GUARD, LANES), F32)
    for ref in (u0, u1, cy):
        for w in range(WIDE):
            ref[w, 0:GUARD, :] = guards
            ref[w, ROWS - GUARD:, :] = guards
    for w in range(WIDE):
        kf[0, w, 0:GUARD, :] = guards
        kf[0, w, ROWS - GUARD:, :] = guards
    for j in range(half):
        for ref in (kc, ccy):
            ref[j, 0:GUARD, :] = guards
            ref[j, C_ROWS - GUARD:, :] = guards
        for m in range(KRYLOV):
            basis[m, j, 0:GUARD, :] = guards
            basis[m, j, C_ROWS - GUARD:, :] = guards

    def clear(ref):
        ref[...] = jnp.zeros(ref.shape, ref.dtype)

    @pl.when(p == 0)
    def _():
        clear(low)

    @pl.when(p == n_patch - 1)
    def _():
        clear(high)

    def outside(planes):
        for w in planes:
            def wipe(i, w=w):
                rows = at_tile(i, 0)
                kf[0, w, rows, :] = zero
                kf[1, w, rows, :] = zero
                u1[w, rows, :] = zero

            loop(ROWS // 8, wipe)
            for a in range(2):
                for ref in (low, high):
                    ref[a, w] = jnp.zeros((HALO, LANES), F32)

    @pl.when(g < 2)
    def _():
        outside((0, 1))

    @pl.when(g < 1)
    def _():
        outside((2, 3))

    @pl.when(g > n_grp - 3)
    def _():
        outside((8, 9))

    @pl.when(g > n_grp - 2)
    def _():
        outside((6, 7))

    pl.semaphore_wait(barrier, n_patch + n_grp + 6)

    def remote(src, dst, send, recv, peer):
        return pltpu.make_async_remote_copy(
            src_ref=src, dst_ref=dst, send_sem=send, recv_sem=recv, device_id=peer, device_id_type=MESH
        )

    first = []
    for dp, source, landing in ((0, own, kf), (1, last, low), (-1, own, high)):
        for dg in (-1, 1, -2, 2, 0):
            if dp == 0 and dg == 0:
                continue
            at = 4 - 2 * dg
            if abs(dg) == 2:
                w = 1 if dg == 2 else 0
                src, dst = source.at[0, w], landing.at[0, at + w]
                if dp == 0:
                    dst = landing.at[0, at + w, FIRST:FIRST + OWN, :]
                elif dp == -1:
                    src = source.at[0, w, 0:HALO, :]
            else:
                src, dst = source, landing.at[:, at:at + 2]
                if dp == 0:
                    dst = landing.at[:, at:at + 2, FIRST:FIRST + OWN, :]
                elif dp == -1:
                    src = source.at[:, :, 0:HALO, :]
            peer = (lax.rem(p + dp + n_patch, n_patch), lax.rem(g + dg + n_grp, n_grp))
            i = len(first)
            first.append((dp, dg, remote(src, dst, p_send.at[i], p_recv.at[i], peer)))

    def start(copies):
        for dp, dg, copy in copies:
            @pl.when(inside(dp, dg))
            def _(copy=copy):
                copy.start()

    def arrive(copies):
        for dp, dg, copy in copies:
            @pl.when(inside(-dp, -dg))
            def _(copy=copy):
                copy.wait_recv()

    def leave(copies):
        for dp, dg, copy in copies:
            @pl.when(inside(dp, dg))
            def _(copy=copy):
                copy.wait_send()

    start(first)
    arrive(first)

    def extend(a, w):
        kf[a, w, GUARD:FIRST, :] = low[a, w]
        upper = high[a, w]
        middle = slice(FIRST + PATCH, FIRST + PATCH + HALO)
        kf[a, w, middle, :] = jnp.where(two, kf[a, w, middle, :], upper)
        kf[a, w, FIRST + OWN:FIRST + OWN + HALO, :] = jnp.where(two, upper, 0.0)

    for w in range(1, 9):
        extend(0, w)
    for w in range(2, 8):
        extend(1, w)

    inner = slice(GUARD, GUARD + EXT)
    second = []
    for dg, src, dst in ((2, (0, 4), (0, 0)), (-2, (0, 5), (0, 9)), (2, (1, 5), (1, 1)), (-2, (1, 4), (1, 8))):
        i = len(second)
        peer = (p, lax.rem(g + dg + n_grp, n_grp))
        second.append((0, dg, remote(
            kf.at[src[0], src[1], inner, :], kf.at[dst[0], dst[1], inner, :], b_send.at[i], b_recv.at[i], peer)))

    def halve(slot, scale):
        def fold(i):
            s = total[pl.ds(GUARD + 16 * i, 8, stride=2), :] + total[pl.ds(GUARD + 16 * i + 1, 8, stride=2), :]
            coarse[at_tile(i, 0), :] = scale * (s + jnp.where(even, lane_roll(s, -1), lane_roll(s, 1)))

        loop(C_TILES, fold)

        def pack(i):
            value = jnp.where(even, coarse[at_tile(i, 0), :], coarse[at_tile(i, C_SKIP), :])
            packed[slot, at_tile(i, 0), :] = value
            gathered[slot, g, at_tile(i, 0), :] = value

        loop(C_SENT // 8, pack)
        return [
            remote(packed.at[slot], gathered.at[slot, g], c_send.at[slot, dg], c_recv.at[slot, dg],
                   (p, lax.rem(g + dg, n_grp)))
            for dg in range(1, n_grp)
        ]

    def unpack(slot, write):
        def upper(i):
            for j in range(half):
                a, b = gathered[slot, j, at_tile(i, 0), :], gathered[slot, j + half, at_tile(i, 0), :]
                write(j, at_tile(i, GUARD), jnp.where(even, a, lane_roll(b, 1)))

        def lower(i):
            for j in range(half):
                a, b = gathered[slot, j, at_tile(i, 8), :], gathered[slot, j + half, at_tile(i, 8), :]
                write(j, at_tile(i, GUARD + C_SENT), jnp.where(even, lane_roll(a, -1), b))

        loop(C_SENT // 8, upper)
        loop((C_EXT - C_SENT) // 8, lower)

    def sum_conduct(i):
        rows = at_tile(i, GUARD)
        total[rows, :] = kf[0, 4, rows, :] + kf[0, 5, rows, :]

    loop(TILES, sum_conduct)
    conduct_out = halve(0, 0.125)
    for copy in conduct_out:
        copy.start()

    def joined(a, b):
        return jnp.where((a > 0) & (b > 0), 0.5 * (a + b), 0.0)

    def set_diag(planes):
        def body(i):
            rows, before, after = at_tile(i, GUARD), at_tile(i, GUARD - 1), at_tile(i, GUARD + 1)
            for w in planes:
                k = kf[0, w, rows, :]
                near = kf[0, w - 1, rows, :] + kf[0, w + 1, rows, :] + kf[0, w, before, :] + kf[0, w, after, :]
                near = near + jnp.where(lane == LANES - 1, 0.0, lane_roll(k, -1))
                near = near + jnp.where(lane == 0, 0.0, lane_roll(k, 1))
                d = 3.0 * k + 0.5 * near
                diag[w, rows, :] = jnp.where(k > 0, d, 0.0)
                gain[w, rows, :] = jnp.where(k > 0, 0.8 / d, 0.0)

        loop(TILES, body)

    def set_weights(planes, between):
        def body(i):
            rows, after = at_tile(i, GUARD), at_tile(i, GUARD + 1)
            for w in between:
                cx[w, rows, :] = joined(kf[0, w, rows, :], kf[0, w + 1, rows, :])
            for w in planes:
                k = kf[0, w, rows, :]
                cy[w, rows, :] = joined(k, kf[0, w, after, :])
                cz[w, rows, :] = jnp.where(lane == LANES - 1, 0.0, joined(k, lane_roll(k, -1)))

        loop(TILES, body)

    def neighbours(u, i, planes):
        rows, before, after = at_tile(i, GUARD), at_tile(i, GUARD - 1), at_tile(i, GUARD + 1)
        centre = {w: u[w, rows, :] for w in range(planes[0] - 1, planes[-1] + 2)}
        result = {}
        for w in planes:
            z = cz[w, rows, :]
            s = cx[w, rows, :] * centre[w + 1] + cx[w - 1, rows, :] * centre[w - 1]
            s = s + cy[w, rows, :] * u[w, after, :] + cy[w, before, :] * u[w, before, :]
            s = s + z * lane_roll(centre[w], -1) + lane_roll(z * centre[w], 1)
            result[w] = s
        return rows, centre, result

    def sweep(src, dst, planes):
        def body(i):
            rows, centre, near = neighbours(src, i, planes)
            for w in planes:
                dst[w, rows, :] = 0.2 * centre[w] + gain[w, rows, :] * (kf[1, w, rows, :] + near[w])

        loop(TILES, body)

    def residual(src):
        def body(i):
            rows, centre, near = neighbours(src, i, (4, 5))
            r = [kf[1, w, rows, :] - diag[w, rows, :] * centre[w] + near[w] for w in (4, 5)]
            total[rows, :] = r[0] + r[1]

        loop(TILES, body)

    def set_coarse():
        def body(i):
            rows, before, after = at_tile(i, GUARD), at_tile(i, GUARD - 1), at_tile(i, GUARD + 1)
            k = [kc[j, rows, :] for j in range(half)]
            for j in range(half):
                beyond = k[j + 1] if j + 1 < half else jnp.where(even, lane_roll(k[0], -1), 0.0)
                ahead = k[j - 1] if j else jnp.where(even, 0.0, lane_roll(k[half - 1], 1))
                right = jnp.where(lane >= LANES - 2, 0.0, lane_roll(k[j], -2))
                left = jnp.where(lane < 2, 0.0, lane_roll(k[j], 2))
                up = kc[j, after, :]
                near = beyond + ahead + right + left + up + kc[j, before, :]
                cdiag[j, rows, :] = jnp.where(k[j] > 0, 3.0 * k[j] + 0.5 * near, 0.0)
                ccx[j, rows, :] = joined(k[j], beyond)
                ccy[j, rows, :] = joined(k[j], up)
                ccz[j, rows, :] = joined(k[j], right)

        loop(C_TILES, body)

    def krylov(cycle):
        sums = []
        for m in range(KRYLOV):
            def body(i, carry, m=m):
                rows, before, after = at_tile(i, GUARD), at_tile(i, GUARD - 1), at_tile(i, GUARD + 1)
                at = row + 8 * i
                mine = (at >= HALO // 2) & (at < HALO // 2 + PATCH // 2 * count)
                v = [basis[m, j, rows, :] for j in range(half)]
                square, cross = carry
                for j in range(half):
                    x, z = ccx[j, rows, :], ccz[j, rows, :]
                    s = x * v[j + 1] if j + 1 < half else x * lane_roll(v[0], -1)
                    if j:
                        s = s + ccx[j - 1, rows, :] * v[j - 1]
                    else:
                        s = s + lane_roll(ccx[half - 1, rows, :] * v[half - 1], 1)
                    s = s + ccy[j, rows, :] * basis[m, j, after, :] + ccy[j, before, :] * basis[m, j, before, :]
                    s = s + z * lane_roll(v[j], -2) + lane_roll(z * v[j], 2)
                    mapped = cdiag[j, rows, :] * v[j] - s
                    if m + 1 < KRYLOV:
                        basis[m + 1, j, rows, :] = mapped
                    masked = jnp.where(mine, v[j], 0.0)
                    square = square + masked * v[j]
                    cross = cross + masked * mapped
                return square, cross

            sums.extend(lax.fori_loop(0, C_TILES, body, (zero, zero)))
        line = jnp.zeros((1, LANES), F32)
        for m, value in enumerate(sums):
            line = jnp.where(lane[0:1] == m, jnp.sum(value), line)
        part[cycle] = line
        parts[cycle, p] = line

        def addressed(i):
            return remote(part.at[cycle], parts.at[cycle, p], s_send.at[cycle, i], s_recv.at[cycle, i],
                          (lax.rem(p + i + 1, n_patch), g))

        loop(n_patch - 1, lambda i: addressed(i).start())
        return addressed

    def coefficients(cycle, addressed):
        loop(n_patch - 1, lambda i: addressed(i).wait_recv())
        whole = jnp.sum(parts[cycle], axis=0)
        moment = [jnp.broadcast_to(whole[:, m:m + 1], (8, LANES)) for m in range(2 * KRYLOV)]
        matrix = [[moment[i + j + 1] for j in range(KRYLOV)] for i in range(KRYLOV)]
        right = moment[:KRYLOV]
        inverse = []
        for i in range(KRYLOV):
            pivot = matrix[i][i]
            inverse.append(jnp.where(pivot > 0, 1.0 / pivot, 0.0))
            for j in range(i + 1, KRYLOV):
                factor = matrix[i][j] * inverse[i]
                for l in range(j, KRYLOV):
                    matrix[j][l] = matrix[j][l] - factor * matrix[i][l]
                right[j] = right[j] - factor * right[i]
        answer = [None] * KRYLOV
        for i in reversed(range(KRYLOV)):
            value = right[i]
            for j in range(i + 1, KRYLOV):
                value = value - matrix[i][j] * answer[j]
            answer[i] = value * inverse[i]
        return answer

    def correct(u, answer, slabs):
        for s in slabs:
            at = g + s - 2
            valid = (at >= 0) & (at < n_grp)
            at = lax.rem(at + n_grp, n_grp)
            j, odd = lax.rem(at, half), at // half

            def body(i, s=s, valid=valid, j=j, odd=odd):
                value = zero
                for m in range(KRYLOV):
                    value = value + answer[m] * basis[m, j, at_tile(i, GUARD), :]
                moved = jnp.where(odd == 0, lane_roll(value, 1), lane_roll(value, -1))
                value = jnp.where(lane % 2 == odd, value, moved)
                value = jnp.where(valid, value, 0.0)
                for w in (2 * s, 2 * s + 1):
                    for a in range(2):
                        rows = pl.ds(GUARD + 16 * i + a, 8, stride=2)
                        u[w, rows, :] = u[w, rows, :] + value

            loop(C_TILES, body)

    def to_basis(j, rows, value):
        basis[0, j, rows, :] = value

    def to_conduct(j, rows, value):
        kc[j, rows, :] = value

    set_diag(range(2, 8))
    start(second)
    set_weights(range(3, 7), range(2, 7))

    def sweep_zero(i):
        rows = at_tile(i, GUARD)
        for w in range(2, 8):
            u0[w, rows, :] = gain[w, rows, :] * kf[1, w, rows, :]

    loop(TILES, sweep_zero)
    sweep(u0, u1, range(3, 7))
    residual(u1)
    first_out = halve(1, 0.5)
    for copy in first_out:
        copy.start()
    for copy in conduct_out:
        copy.wait_recv()
    unpack(0, to_conduct)
    set_coarse()
    for copy in first_out:
        copy.wait_recv()

    third = []
    for dg, src, dst in ((1, slice(4, 5), slice(2, 3)), (-1, slice(5, 6), slice(7, 8)),
                         (2, slice(4, 6), slice(0, 2)), (-2, slice(4, 6), slice(8, 10))):
        i = len(third)
        peer = (p, lax.rem(g + dg + n_grp, n_grp))
        third.append((0, dg, remote(u1.at[src, inner, :], u1.at[dst, inner, :], w_send.at[i], w_recv.at[i], peer)))
    start(third)
    unpack(1, to_basis)
    addressed = krylov(0)
    arrive(second)
    set_diag((1, 8))
    set_weights((1, 2, 7, 8), (0, 1, 7, 8))
    arrive(third)
    leave(third)
    answer = coefficients(0, addressed)
    correct(u1, answer, range(5))
    sweep(u1, u0, range(1, 9))

    sweep(u0, u1, range(2, 8))
    sweep(u1, u0, range(3, 7))
    residual(u0)
    second_out = halve(2, 0.5)
    for copy in second_out:
        copy.start()
    for copy in second_out:
        copy.wait_recv()
    unpack(2, to_basis)
    addressed_again = krylov(1)
    answer = coefficients(1, addressed_again)
    correct(u0, answer, range(1, 4))
    sweep(u0, u1, range(4, 6))

    def finish(i):
        for w in range(2):
            used = row + 8 * i < PATCH * count
            out_ref[w, at_tile(i, 0), :] = jnp.where(used, u1[4 + w, at_tile(i, FIRST), :], 0.0)

    loop(OWN // 8, finish)

    leave(first)
    leave(second)
    for copy in conduct_out + first_out + second_out:
        copy.wait_send()
    loop(n_patch - 1, lambda i: addressed(i).wait_send())
    loop(n_patch - 1, lambda i: addressed_again(i).wait_send())


def solution(mesh):
    n_patch, n_grp = mesh.shape["patch"], mesh.shape["grp"]
    half = n_grp // 2

    def per_device(right_side, coefficient, row_counts):
        fine = pltpu.VMEM((WIDE, ROWS, LANES), F32)
        level = pltpu.VMEM((half, C_ROWS, LANES), F32)
        dma = pltpu.SemaphoreType.DMA
        return pl.pallas_call(
            functools.partial(kernel, n_patch, n_grp),
            out_shape=jax.ShapeDtypeStruct(right_side.shape, F32),
            in_specs=[
                pl.BlockSpec(memory_space=pltpu.VMEM),
                pl.BlockSpec(memory_space=pltpu.VMEM),
                pl.BlockSpec(memory_space=pltpu.SMEM),
            ],
            out_specs=pl.BlockSpec(memory_space=pltpu.VMEM),
            scratch_shapes=[
                pltpu.VMEM((2, 2, OWN, LANES), F32),
                pltpu.VMEM((2, 2, HALO, LANES), F32),
                pltpu.VMEM((2, WIDE, HALO, LANES), F32),
                pltpu.VMEM((2, WIDE, HALO, LANES), F32),
                pltpu.VMEM((2, WIDE, ROWS, LANES), F32),
                fine, fine, fine, fine, fine, fine, fine,
                pltpu.VMEM((ROWS, LANES), F32),
                pltpu.VMEM((C_EXT, LANES), F32),
                pltpu.VMEM((3, C_SENT, LANES), F32),
                pltpu.VMEM((3, n_grp, C_SENT, LANES), F32),
                level, level, level, level, level,
                pltpu.VMEM((KRYLOV, half, C_ROWS, LANES), F32),
                pltpu.VMEM((CYCLES, 1, LANES), F32),
                pltpu.VMEM((CYCLES, n_patch, 1, LANES), F32),
                dma((14,)), dma((14,)), dma((4,)), dma((4,)), dma((4,)), dma((4,)),
                dma((3, n_grp)), dma((3, n_grp)),
                dma((CYCLES, n_patch - 1)), dma((CYCLES, n_patch - 1)),
            ],
            compiler_params=pltpu.CompilerParams(
                collective_id=0, has_side_effects=True, vmem_limit_bytes=40 << 20
            ),
        )(right_side, coefficient, row_counts)

    return jax.shard_map(
        per_device,
        mesh=mesh,
        in_specs=(P("grp", "patch", None), P("grp", "patch", None), P("patch")),
        out_specs=P("grp", "patch", None),
        check_vma=False,
    )
```

time: 1680 us -> 90.4 us (0.05)
  blocking collectives: 1390 us -> 0 us
  starting transfers between devices: 175 us -> 0 us
  Pallas kernels: 0 us -> 87.2 us
  waiting for transfers between devices: 45 us -> 0 us
  other arithmetic: 23.8 us -> 0 us
  between operations: 21.1 us -> 0.67 us
    psum x14 -> x0, blocking collectives: 1390 us -> none  [coarse_total(): return lax.psum(value, ('patch', 'grp'))]
    ppermute x72 -> x0, starting transfers between devices: 175 us -> none  [the longest x36 74.4 us: shifted_2(): lax.ppermute(value, axis, [(source, source + steps) for source in range(i...]
    pallas_call x0 -> x1, Pallas kernels: none -> 87.2 us  [per_device(): pl.pallas_call(functools.partial(kernel, n_patch, n_grp), out_shape=jax.S...]
    ppermute x72 -> x0, waiting for transfers between devices: 45 us -> none  [the longest x36 24.5 us: shifted_2(): lax.ppermute(value, axis, [(source, source + steps) for source in range(i...]
    reduce_sum x22 -> x0, other arithmetic: 20.9 us -> none  [the longest x6 9.67 us: restrict(): return 0.5 * jnp.sum(blocks, axis=(1, 3, 5))]
  transfers between devices with their start and end apart: 72 -> 0, of which waited for: 14 -> 0; matrix products, arithmetic and copies ran while one was open for 1% -> 0% of each run, Pallas kernels for 0% -> 0%
where the time goes in v1:
time: 90.4 us; the launch traced here: 90.2 us
  Pallas kernels  87.2 us (96%)
  local copies, waits for them, and re-layouts  2.33 us (3%)
    pallas_call x1, Pallas kernels, per_device(): pl.pallas_call(functools.partial(kernel, n_patch, n_grp), out_shape=jax.S...  87.2 us
    unnamed x5, local copies, waits for them, and re-layouts  2.33 us

profile of v1, /device:TPU:1, one launch (start us, length us, event | category | flops | bytes accessed | tf_op | source)
XLA Modules:
  0.0 90.2 jit_solution(6143695238026984307)
XLA Ops:
  0.7 0.0 copy-start
  0.7 0.8 copy-done
  1.5 0.0 copy-start.1
  1.5 0.8 copy-done.1
  2.3 87.2 %shard_map.37 = f32[2,128,128]{2,1,0:T(8,128)S(1)} custom-call(bf16[2,128,128]{2,1,0:T(8,128)(2,1)S(1)} %copy-done, bf16[2,128,128]{2,1,0:T(8,128)(2,1)S(1)} %copy-done.1, s32[1]{0:T(128)S(6)} %copy.5.count_ref), custom_call_target="tpu_custom_call" | custom-call | tf_op jit(solution)/shard_map/pallas_call | solution.py:502
  89.5 0.7 copy.6
Async XLA Ops:
  0.7 0.8 copy-start
  1.5 0.8 copy-start.1

commit v2 on v1

--- a/solution.py
+++ b/solution.py
@@ -26,18 +26,26 @@
 C_SENT = 48
 C_SKIP = C_EXT - C_SENT
 F32 = jnp.float32
+GROUP = 22
+C_GROUP = 11
 
 
 def lane_roll(x, steps):
     return pltpu.roll(x, steps % LANES, axis=1)
 
 
-def loop(count, body):
+def loop(count, body, group=1):
+    if group >= count:
+        for i in range(count):
+            body(i)
+        return
+
     def step(i, carry):
-        body(i)
+        for k in range(group):
+            body(group * i + k)
         return carry
 
-    lax.fori_loop(0, count, step, 0)
+    lax.fori_loop(0, count // group, step, 0)
 
 
 def at_tile(i, offset):
@@ -220,14 +228,14 @@
             s = total[pl.ds(GUARD + 16 * i, 8, stride=2), :] + total[pl.ds(GUARD + 16 * i + 1, 8, stride=2), :]
             coarse[at_tile(i, 0), :] = scale * (s + jnp.where(even, lane_roll(s, -1), lane_roll(s, 1)))
 
-        loop(C_TILES, fold)
+        loop(C_TILES, fold, C_GROUP)
 
         def pack(i):
             value = jnp.where(even, coarse[at_tile(i, 0), :], coarse[at_tile(i, C_SKIP), :])
             packed[slot, at_tile(i, 0), :] = value
             gathered[slot, g, at_tile(i, 0), :] = value
 
-        loop(C_SENT // 8, pack)
+        loop(C_SENT // 8, pack, C_GROUP)
         return [
             remote(packed.at[slot], gathered.at[slot, g], c_send.at[slot, dg], c_recv.at[slot, dg],
                    (p, lax.rem(g + dg, n_grp)))
@@ -245,14 +253,14 @@
                 a, b = gathered[slot, j, at_tile(i, 8), :], gathered[slot, j + half, at_tile(i, 8), :]
                 write(j, at_tile(i, GUARD + C_SENT), jnp.where(even, lane_roll(a, -1), b))
 
-        loop(C_SENT // 8, upper)
-        loop((C_EXT - C_SENT) // 8, lower)
+        loop(C_SENT // 8, upper, C_GROUP)
+        loop((C_EXT - C_SENT) // 8, lower, C_GROUP)
 
     def sum_conduct(i):
         rows = at_tile(i, GUARD)
         total[rows, :] = kf[0, 4, rows, :] + kf[0, 5, rows, :]
 
-    loop(TILES, sum_conduct)
+    loop(TILES, sum_conduct, GROUP)
     conduct_out = halve(0, 0.125)
     for copy in conduct_out:
         copy.start()
@@ -272,7 +280,7 @@
                 diag[w, rows, :] = jnp.where(k > 0, d, 0.0)
                 gain[w, rows, :] = jnp.where(k > 0, 0.8 / d, 0.0)
 
-        loop(TILES, body)
+        loop(TILES, body, GROUP)
 
     def set_weights(planes, between):
         def body(i):
@@ -284,7 +292,7 @@
                 cy[w, rows, :] = joined(k, kf[0, w, after, :])
                 cz[w, rows, :] = jnp.where(lane == LANES - 1, 0.0, joined(k, lane_roll(k, -1)))
 
-        loop(TILES, body)
+        loop(TILES, body, GROUP)
 
     def neighbours(u, i, planes):
         rows, before, after = at_tile(i, GUARD), at_tile(i, GUARD - 1), at_tile(i, GUARD + 1)
@@ -304,7 +312,7 @@
             for w in planes:
                 dst[w, rows, :] = 0.2 * centre[w] + gain[w, rows, :] * (kf[1, w, rows, :] + near[w])
 
-        loop(TILES, body)
+        loop(TILES, body, GROUP)
 
     def residual(src):
         def body(i):
@@ -312,7 +320,7 @@
             r = [kf[1, w, rows, :] - diag[w, rows, :] * centre[w] + near[w] for w in (4, 5)]
             total[rows, :] = r[0] + r[1]
 
-        loop(TILES, body)
+        loop(TILES, body, GROUP)
 
     def set_coarse():
         def body(i):
@@ -330,7 +338,7 @@
                 ccy[j, rows, :] = joined(k[j], up)
                 ccz[j, rows, :] = joined(k[j], right)
 
-        loop(C_TILES, body)
+        loop(C_TILES, body, C_GROUP)
 
     def krylov(cycle):
         sums = []
@@ -358,7 +366,13 @@
                     cross = cross + masked * mapped
                 return square, cross
 
-            sums.extend(lax.fori_loop(0, C_TILES, body, (zero, zero)))
+            if C_GROUP >= C_TILES:
+                carry = (zero, zero)
+                for i in range(C_TILES):
+                    carry = body(i, carry)
+                sums.extend(carry)
+            else:
+                sums.extend(lax.fori_loop(0, C_TILES, body, (zero, zero)))
         line = jnp.zeros((1, LANES), F32)
         for m, value in enumerate(sums):
             line = jnp.where(lane[0:1] == m, jnp.sum(value), line)
@@ -414,7 +428,7 @@
                         rows = pl.ds(GUARD + 16 * i + a, 8, stride=2)
                         u[w, rows, :] = u[w, rows, :] + value
 
-            loop(C_TILES, body)
+            loop(C_TILES, body, C_GROUP)
 
     def to_basis(j, rows, value):
         basis[0, j, rows, :] = value
@@ -431,7 +445,7 @@
         for w in range(2, 8):
             u0[w, rows, :] = gain[w, rows, :] * kf[1, w, rows, :]
 
-    loop(TILES, sweep_zero)
+    loop(TILES, sweep_zero, GROUP)
     sweep(u0, u1, range(3, 7))
     residual(u1)
     first_out = halve(1, 0.5)

time: 90.4 us -> 64 us (0.71)
  Pallas kernels: 87.2 us -> 60.8 us
    pallas_call x1, Pallas kernels: 87.2 us -> 60.8 us  [per_device(): pl.pallas_call(functools.partial(kernel, n_patch, n_grp), out_shape=jax.S...]
where the time goes in v2:
time: 64 us; the launch traced here: 63.8 us
  Pallas kernels  60.8 us (95%)
  local copies, waits for them, and re-layouts  2.33 us (4%)
  between operations  0.67 us (1%)
    pallas_call x1, Pallas kernels, per_device(): pl.pallas_call(functools.partial(kernel, n_patch, n_grp), out_shape=jax.S...  60.8 us
    unnamed x5, local copies, waits for them, and re-layouts  2.33 us

profile of v2, /device:TPU:1, one launch (start us, length us, event | category | flops | bytes accessed | tf_op | source)
XLA Modules:
  0.0 63.8 jit_solution(15699551698439957010)
XLA Ops:
  0.7 0.0 copy-start
  0.7 0.8 %copy-done = bf16[2,128,128]{2,1,0:T(8,128)(2,1)S(1)} copy-done((bf16[2,128,128]{2,1,0:T(8,128)(2,1)S(1)}, bf16[2,128,128]{2,1,0:T(8,128)(2,1)}, u32[]{:S(2)}) %copy-start) | copy-done | bytes 65560
  1.5 0.0 copy-start.1
  1.5 0.8 %copy-done.1 = bf16[2,128,128]{2,1,0:T(8,128)(2,1)S(1)} copy-done((bf16[2,128,128]{2,1,0:T(8,128)(2,1)S(1)}, bf16[2,128,128]{2,1,0:T(8,128)(2,1)}, u32[]{:S(2)}) %copy-start.1) | copy-done | bytes 65560
  2.3 60.8 %shard_map.37 = f32[2,128,128]{2,1,0:T(8,128)S(1)} custom-call(bf16[2,128,128]{2,1,0:T(8,128)(2,1)S(1)} %copy-done, bf16[2,128,128]{2,1,0:T(8,128)(2,1)S(1)} %copy-done.1, s32[1]{0:T(128)S(6)} %copy.5.count_ref), custom_call_target="tpu_custom_call" | custom-call | tf_op jit(solution)/shard_map/pallas_call | solution.py:516
  63.1 0.7 %copy.6 = f32[2,128,128]{2,1,0:T(8,128)} copy(f32[2,128,128]{2,1,0:T(8,128)S(1)} %shard_map.37) | data formatting | bytes 262144
Async XLA Ops:
  0.7 0.8 %copy-start = (bf16[2,128,128]{2,1,0:T(8,128)(2,1)S(1)}, bf16[2,128,128]{2,1,0:T(8,128)(2,1)}, u32[]{:S(2)}) copy-start(bf16[2,128,128]{2,1,0:T(8,128)(2,1)} %rs_ref.1) | copy-start | bytes 196612
  1.5 0.8 %copy-start.1 = (bf16[2,128,128]{2,1,0:T(8,128)(2,1)S(1)}, bf16[2,128,128]{2,1,0:T(8,128)(2,1)}, u32[]{:S(2)}) copy-start(bf16[2,128,128]{2,1,0:T(8,128)(2,1)} %cf_ref.1) | copy-start | bytes 196612

commit v3 on v1

--- a/solution.py
+++ b/solution.py
@@ -11,6 +11,7 @@
 CYCLES = 2
 KRYLOV = 4
 PATCH = 64
+CAP = 2
 OWN = 128
 HALO = 24
 EXT = OWN + 2 * HALO
@@ -19,13 +20,16 @@
 FIRST = GUARD + HALO
 WIDE = 10
 LANES = 128
-TILES = EXT // 8
+ALL = range(EXT // 8)
+MOST = range(1, EXT // 8 - 1)
+MINE = range(HALO // 8, (HALO + OWN) // 8)
 C_EXT = EXT // 2
 C_ROWS = C_EXT + 2 * GUARD
-C_TILES = C_EXT // 8
+C_ALL = range(C_EXT // 8)
+C_MOST = range(1, C_EXT // 8 - 1)
 C_SENT = 48
-C_SKIP = C_EXT - C_SENT
 F32 = jnp.float32
+SIDE = 8
 
 
 def lane_roll(x, steps):
@@ -40,19 +44,32 @@
     lax.fori_loop(0, count, step, 0)
 
 
+def each(tiles, body):
+    for i in tiles:
+        body(i)
+
+
+def farthest_first(i):
+    return SIDE // 2 + jnp.where(i % 2 == 0, i // 2, -((i + 1) // 2))
+
+
 def at_tile(i, offset):
     return pl.ds(offset + 8 * i, 8)
 
 
-def kernel(n_patch, n_grp, rs_ref, cf_ref, count_ref, out_ref,
-           own, last, low, high, kf, gain, diag, cx, cy, cz, u0, u1, total, coarse, packed, gathered,
+def kernel(n_patch, n_grp, rs_hbm, cf_hbm, count_hbm, out_ref,
+           rs_ref, cf_ref, count_ref, in_sem, own, last, low, high, kf, gain, diag, cx, cy, cz, u0, u1, total, coarse, packed, gathered,
            kc, ccx, ccy, ccz, cdiag, basis, part, parts,
            p_send, p_recv, b_send, b_recv, w_send, w_recv, c_send, c_recv, s_send, s_recv):
     half = n_grp // 2
     p = lax.axis_index("patch")
     g = lax.axis_index("grp")
-    count = count_ref[0]
-    two = count >= 2
+    loads = [
+        pltpu.make_async_copy(src, dst, in_sem.at[i])
+        for i, (src, dst) in enumerate(((count_hbm, count_ref), (cf_hbm, cf_ref), (rs_hbm, rs_ref)))
+    ]
+    for copy in loads:
+        copy.start()
 
     lane = lax.broadcasted_iota(jnp.int32, (8, LANES), 1)
     row = lax.broadcasted_iota(jnp.int32, (8, LANES), 0)
@@ -75,17 +92,20 @@
         pl.semaphore_signal(barrier, inc=1, device_id=peer, device_id_type=MESH)
 
     loop(n_patch - 1, greet)
+    for copy in loads:
+        copy.wait()
+    count = count_ref[0]
+    two = count >= 2
 
     for a, ref in ((0, cf_ref), (1, rs_ref)):
         for w in range(2):
-            def stage(i, a=a, ref=ref, w=w):
-                rows = pl.ds(16 * i, 16)
-                at = lax.broadcasted_iota(jnp.int32, (16, LANES), 0) + 16 * i
-                value = jnp.where(at < PATCH * count, ref[w, rows, :].astype(F32), 0.0)
+            for half_rows in range(CAP):
+                rows = slice(PATCH * half_rows, PATCH * (half_rows + 1))
+                value = ref[w, rows, :].astype(F32)
+                if half_rows:
+                    value = jnp.where(two, value, 0.0)
                 own[a, w, rows, :] = value
-                kf[a, 4 + w, pl.ds(FIRST + 16 * i, 16), :] = value
-
-            loop(OWN // 16, stage)
+                kf[a, 4 + w, FIRST + PATCH * half_rows:FIRST + PATCH * (half_rows + 1), :] = value
             last[a, w] = jnp.where(two, own[a, w, OWN - HALO:, :], own[a, w, PATCH - HALO:PATCH, :])
 
     guards = jnp.zeros((GUARD, LANES), F32)
@@ -152,27 +172,22 @@
         )
 
     first = []
-    for dp, source, landing in ((0, own, kf), (1, last, low), (-1, own, high)):
-        for dg in (-1, 1, -2, 2, 0):
-            if dp == 0 and dg == 0:
-                continue
-            at = 4 - 2 * dg
-            if abs(dg) == 2:
-                w = 1 if dg == 2 else 0
-                src, dst = source.at[0, w], landing.at[0, at + w]
+    for a in range(2):
+        for dp, source, landing in ((0, own, kf), (1, last, low), (-1, own, high)):
+            for dg in (-2, 2, -1, 1, 0):
+                if (dp == 0 and dg == 0) or (a == 1 and abs(dg) == 2):
+                    continue
+                at = 4 - 2 * dg
+                w = {2: slice(1, 2), -2: slice(0, 1)}.get(dg, slice(0, 2))
+                src, dst = source.at[a, w], landing.at[a, at + w.start:at + w.stop]
                 if dp == 0:
-                    dst = landing.at[0, at + w, FIRST:FIRST + OWN, :]
+                    dst = landing.at[a, at + w.start:at + w.stop, FIRST:FIRST + OWN, :]
                 elif dp == -1:
-                    src = source.at[0, w, 0:HALO, :]
-            else:
-                src, dst = source, landing.at[:, at:at + 2]
-                if dp == 0:
-                    dst = landing.at[:, at:at + 2, FIRST:FIRST + OWN, :]
-                elif dp == -1:
-                    src = source.at[:, :, 0:HALO, :]
-            peer = (lax.rem(p + dp + n_patch, n_patch), lax.rem(g + dg + n_grp, n_grp))
-            i = len(first)
-            first.append((dp, dg, remote(src, dst, p_send.at[i], p_recv.at[i], peer)))
+                    src = source.at[a, w, 0:HALO, :]
+                peer = (lax.rem(p + dp + n_patch, n_patch), lax.rem(g + dg + n_grp, n_grp))
+                i = len(first)
+                first.append((dp, dg, remote(src, dst, p_send.at[i], p_recv.at[i], peer)))
+    conduct_halo, source_halo = first[:14], first[14:]
 
     def start(copies):
         for dp, dg, copy in copies:
@@ -192,8 +207,9 @@
             def _(copy=copy):
                 copy.wait_send()
 
-    start(first)
-    arrive(first)
+    start(conduct_halo)
+    start(source_halo)
+    arrive(conduct_halo)
 
     def extend(a, w):
         kf[a, w, GUARD:FIRST, :] = low[a, w]
@@ -204,10 +220,8 @@
 
     for w in range(1, 9):
         extend(0, w)
-    for w in range(2, 8):
-        extend(1, w)
-
-    inner = slice(GUARD, GUARD + EXT)
+
+    inner = slice(GUARD + 8, GUARD + EXT - 8)
     second = []
     for dg, src, dst in ((2, (0, 4), (0, 0)), (-2, (0, 5), (0, 9)), (2, (1, 5), (1, 1)), (-2, (1, 4), (1, 8))):
         i = len(second)
@@ -215,52 +229,62 @@
         second.append((0, dg, remote(
             kf.at[src[0], src[1], inner, :], kf.at[dst[0], dst[1], inner, :], b_send.at[i], b_recv.at[i], peer)))
 
-    def halve(slot, scale):
+    def halve(slot, scale, tiles):
+        top, sent, skip = window(tiles)
+
         def fold(i):
             s = total[pl.ds(GUARD + 16 * i, 8, stride=2), :] + total[pl.ds(GUARD + 16 * i + 1, 8, stride=2), :]
             coarse[at_tile(i, 0), :] = scale * (s + jnp.where(even, lane_roll(s, -1), lane_roll(s, 1)))
 
-        loop(C_TILES, fold)
+        each(tiles, fold)
 
         def pack(i):
-            value = jnp.where(even, coarse[at_tile(i, 0), :], coarse[at_tile(i, C_SKIP), :])
+            value = jnp.where(even, coarse[at_tile(i, top), :], coarse[at_tile(i, top + skip), :])
             packed[slot, at_tile(i, 0), :] = value
             gathered[slot, g, at_tile(i, 0), :] = value
 
-        loop(C_SENT // 8, pack)
+        each(range(sent // 8), pack)
         return [
-            remote(packed.at[slot], gathered.at[slot, g], c_send.at[slot, dg], c_recv.at[slot, dg],
-                   (p, lax.rem(g + dg, n_grp)))
-            for dg in range(1, n_grp)
+            remote(packed.at[slot, 0:sent, :], gathered.at[slot, g, 0:sent, :], c_send.at[slot, dg],
+                   c_recv.at[slot, dg], (p, lax.rem(g + dg, n_grp)))
+            for dg in sorted(range(1, n_grp), key=lambda d: (-min(d, n_grp - d), d))
         ]
 
-    def unpack(slot, write):
+    def window(tiles):
+        rows = 8 * len(tiles)
+        sent = (rows // 2 + 7) // 8 * 8
+        return 8 * tiles[0], sent, rows - sent
+
+    def unpack(slot, write, tiles):
+        top, sent, skip = window(tiles)
+
         def upper(i):
             for j in range(half):
                 a, b = gathered[slot, j, at_tile(i, 0), :], gathered[slot, j + half, at_tile(i, 0), :]
-                write(j, at_tile(i, GUARD), jnp.where(even, a, lane_roll(b, 1)))
+                write(j, at_tile(i, GUARD + top), jnp.where(even, a, lane_roll(b, 1)))
 
         def lower(i):
             for j in range(half):
-                a, b = gathered[slot, j, at_tile(i, 8), :], gathered[slot, j + half, at_tile(i, 8), :]
-                write(j, at_tile(i, GUARD + C_SENT), jnp.where(even, lane_roll(a, -1), b))
-
-        loop(C_SENT // 8, upper)
-        loop((C_EXT - C_SENT) // 8, lower)
+                rows = at_tile(i, sent - skip)
+                a, b = gathered[slot, j, rows, :], gathered[slot, j + half, rows, :]
+                write(j, at_tile(i, GUARD + top + sent), jnp.where(even, lane_roll(a, -1), b))
+
+        each(range(sent // 8), upper)
+        each(range(skip // 8), lower)
 
     def sum_conduct(i):
         rows = at_tile(i, GUARD)
         total[rows, :] = kf[0, 4, rows, :] + kf[0, 5, rows, :]
 
-    loop(TILES, sum_conduct)
-    conduct_out = halve(0, 0.125)
+    each(ALL, sum_conduct)
+    conduct_out = halve(0, 0.125, C_ALL)
     for copy in conduct_out:
         copy.start()
 
     def joined(a, b):
         return jnp.where((a > 0) & (b > 0), 0.5 * (a + b), 0.0)
 
-    def set_diag(planes):
+    def set_diag(planes, tiles):
         def body(i):
             rows, before, after = at_tile(i, GUARD), at_tile(i, GUARD - 1), at_tile(i, GUARD + 1)
             for w in planes:
@@ -272,9 +296,9 @@
                 diag[w, rows, :] = jnp.where(k > 0, d, 0.0)
                 gain[w, rows, :] = jnp.where(k > 0, 0.8 / d, 0.0)
 
-        loop(TILES, body)
-
-    def set_weights(planes, between):
+        each(tiles, body)
+
+    def set_weights(planes, between, tiles):
         def body(i):
             rows, after = at_tile(i, GUARD), at_tile(i, GUARD + 1)
             for w in between:
@@ -284,7 +308,7 @@
                 cy[w, rows, :] = joined(k, kf[0, w, after, :])
                 cz[w, rows, :] = jnp.where(lane == LANES - 1, 0.0, joined(k, lane_roll(k, -1)))
 
-        loop(TILES, body)
+        each(tiles, body)
 
     def neighbours(u, i, planes):
         rows, before, after = at_tile(i, GUARD), at_tile(i, GUARD - 1), at_tile(i, GUARD + 1)
@@ -298,21 +322,21 @@
             result[w] = s
         return rows, centre, result
 
-    def sweep(src, dst, planes):
+    def sweep(src, dst, planes, tiles):
         def body(i):
             rows, centre, near = neighbours(src, i, planes)
             for w in planes:
                 dst[w, rows, :] = 0.2 * centre[w] + gain[w, rows, :] * (kf[1, w, rows, :] + near[w])
 
-        loop(TILES, body)
-
-    def residual(src):
+        each(tiles, body)
+
+    def residual(src, tiles):
         def body(i):
             rows, centre, near = neighbours(src, i, (4, 5))
             r = [kf[1, w, rows, :] - diag[w, rows, :] * centre[w] + near[w] for w in (4, 5)]
             total[rows, :] = r[0] + r[1]
 
-        loop(TILES, body)
+        each(tiles, body)
 
     def set_coarse():
         def body(i):
@@ -330,9 +354,9 @@
                 ccy[j, rows, :] = joined(k[j], up)
                 ccz[j, rows, :] = joined(k[j], right)
 
-        loop(C_TILES, body)
-
-    def krylov(cycle):
+        each(C_ALL, body)
+
+    def krylov(cycle, tiles):
         sums = []
         for m in range(KRYLOV):
             def body(i, carry, m=m):
@@ -358,22 +382,29 @@
                     cross = cross + masked * mapped
                 return square, cross
 
-            sums.extend(lax.fori_loop(0, C_TILES, body, (zero, zero)))
-        line = jnp.zeros((1, LANES), F32)
-        for m, value in enumerate(sums):
-            line = jnp.where(lane[0:1] == m, jnp.sum(value), line)
+            carry = (zero, zero)
+            for i in tiles:
+                carry = body(i, carry)
+            sums.extend(carry)
+        stacked = jnp.concatenate([jnp.sum(value, axis=0, keepdims=True) for value in sums], axis=0)
+        stacked = jnp.where(lane == row, jnp.sum(stacked, axis=1, keepdims=True), 0.0)
+        line = jnp.sum(stacked, axis=0, keepdims=True)
         part[cycle] = line
         parts[cycle, p] = line
 
-        def addressed(i):
-            return remote(part.at[cycle], parts.at[cycle, p], s_send.at[cycle, i], s_recv.at[cycle, i],
-                          (lax.rem(p + i + 1, n_patch), g))
-
-        loop(n_patch - 1, lambda i: addressed(i).start())
-        return addressed
-
-    def coefficients(cycle, addressed):
-        loop(n_patch - 1, lambda i: addressed(i).wait_recv())
+        def send(i):
+            dz, dy = farthest_first(i // SIDE), farthest_first(i % SIDE)
+            peer = (lax.rem(p // SIDE + dz, n_patch // SIDE) * SIDE + lax.rem(p % SIDE + dy, SIDE), g)
+            remote(part.at[cycle], parts.at[cycle, p], s_send.at[cycle], s_recv.at[cycle], peer).start()
+
+        loop(n_patch - 1, send)
+
+    def everyone(cycle):
+        rows = parts.at[cycle, 0:n_patch - 1]
+        return remote(rows, rows, s_send.at[cycle], s_recv.at[cycle], (lax.rem(p + 1, n_patch), g))
+
+    def coefficients(cycle):
+        everyone(cycle).wait_recv()
         whole = jnp.sum(parts[cycle], axis=0)
         moment = [jnp.broadcast_to(whole[:, m:m + 1], (8, LANES)) for m in range(2 * KRYLOV)]
         matrix = [[moment[i + j + 1] for j in range(KRYLOV)] for i in range(KRYLOV)]
@@ -395,7 +426,7 @@
             answer[i] = value * inverse[i]
         return answer
 
-    def correct(u, answer, slabs):
+    def correct(u, answer, slabs, tiles):
         for s in slabs:
             at = g + s - 2
             valid = (at >= 0) & (at < n_grp)
@@ -414,7 +445,7 @@
                         rows = pl.ds(GUARD + 16 * i + a, 8, stride=2)
                         u[w, rows, :] = u[w, rows, :] + value
 
-            loop(C_TILES, body)
+            each(tiles, body)
 
     def to_basis(j, rows, value):
         basis[0, j, rows, :] = value
@@ -422,24 +453,26 @@
     def to_conduct(j, rows, value):
         kc[j, rows, :] = value
 
-    set_diag(range(2, 8))
-    start(second)
-    set_weights(range(3, 7), range(2, 7))
+    set_diag(range(2, 8), ALL)
+    set_weights(range(3, 7), range(2, 7), ALL)
+    arrive(source_halo)
+    for w in range(2, 8):
+        extend(1, w)
 
     def sweep_zero(i):
         rows = at_tile(i, GUARD)
         for w in range(2, 8):
             u0[w, rows, :] = gain[w, rows, :] * kf[1, w, rows, :]
 
-    loop(TILES, sweep_zero)
-    sweep(u0, u1, range(3, 7))
-    residual(u1)
-    first_out = halve(1, 0.5)
+    each(ALL, sweep_zero)
+    sweep(u0, u1, range(3, 7), ALL)
+    residual(u1, ALL)
+    first_out = halve(1, 0.5, C_ALL)
     for copy in first_out:
         copy.start()
     for copy in conduct_out:
         copy.wait_recv()
-    unpack(0, to_conduct)
+    unpack(0, to_conduct, C_ALL)
     set_coarse()
     for copy in first_out:
         copy.wait_recv()
@@ -450,45 +483,43 @@
         i = len(third)
         peer = (p, lax.rem(g + dg + n_grp, n_grp))
         third.append((0, dg, remote(u1.at[src, inner, :], u1.at[dst, inner, :], w_send.at[i], w_recv.at[i], peer)))
+    start(second)
     start(third)
-    unpack(1, to_basis)
-    addressed = krylov(0)
+    unpack(1, to_basis, C_ALL)
+    krylov(0, C_ALL)
+    leave(first)
+    for copy in conduct_out + first_out:
+        copy.wait_send()
     arrive(second)
-    set_diag((1, 8))
-    set_weights((1, 2, 7, 8), (0, 1, 7, 8))
+    set_diag((1, 8), MOST)
+    set_weights((1, 2, 7, 8), (0, 1, 7, 8), MOST)
     arrive(third)
     leave(third)
-    answer = coefficients(0, addressed)
-    correct(u1, answer, range(5))
-    sweep(u1, u0, range(1, 9))
-
-    sweep(u0, u1, range(2, 8))
-    sweep(u1, u0, range(3, 7))
-    residual(u0)
-    second_out = halve(2, 0.5)
+    answer = coefficients(0)
+    correct(u1, answer, range(5), C_ALL)
+    sweep(u1, u0, range(1, 9), MOST)
+
+    sweep(u0, u1, range(2, 8), MOST)
+    sweep(u1, u0, range(3, 7), MOST)
+    residual(u0, MOST)
+    second_out = halve(2, 0.5, C_MOST)
     for copy in second_out:
         copy.start()
     for copy in second_out:
         copy.wait_recv()
-    unpack(2, to_basis)
-    addressed_again = krylov(1)
-    answer = coefficients(1, addressed_again)
-    correct(u0, answer, range(1, 4))
-    sweep(u0, u1, range(4, 6))
-
-    def finish(i):
-        for w in range(2):
-            used = row + 8 * i < PATCH * count
-            out_ref[w, at_tile(i, 0), :] = jnp.where(used, u1[4 + w, at_tile(i, FIRST), :], 0.0)
-
-    loop(OWN // 8, finish)
-
-    leave(first)
+    unpack(2, to_basis, C_MOST)
+    krylov(1, C_MOST)
     leave(second)
-    for copy in conduct_out + first_out + second_out:
+    for copy in second_out:
         copy.wait_send()
-    loop(n_patch - 1, lambda i: addressed(i).wait_send())
-    loop(n_patch - 1, lambda i: addressed_again(i).wait_send())
+    everyone(0).wait_send()
+    answer = coefficients(1)
+    correct(u0, answer, range(1, 4), C_MOST)
+    sweep(u0, u1, range(4, 6), MINE)
+    for w in range(2):
+        out_ref[w, 0:PATCH, :] = u1[4 + w, FIRST:FIRST + PATCH, :]
+        out_ref[w, PATCH:, :] = jnp.where(two, u1[4 + w, FIRST + PATCH:FIRST + OWN, :], 0.0)
+    everyone(1).wait_send()
 
 
 def solution(mesh):
@@ -503,12 +534,16 @@
             functools.partial(kernel, n_patch, n_grp),
             out_shape=jax.ShapeDtypeStruct(right_side.shape, F32),
             in_specs=[
-                pl.BlockSpec(memory_space=pltpu.VMEM),
-                pl.BlockSpec(memory_space=pltpu.VMEM),
-                pl.BlockSpec(memory_space=pltpu.SMEM),
+                pl.BlockSpec(memory_space=pltpu.HBM),
+                pl.BlockSpec(memory_space=pltpu.HBM),
+                pl.BlockSpec(memory_space=pltpu.HBM),
             ],
             out_specs=pl.BlockSpec(memory_space=pltpu.VMEM),
             scratch_shapes=[
+                pltpu.VMEM(right_side.shape, right_side.dtype),
+                pltpu.VMEM(coefficient.shape, coefficient.dtype),
+                pltpu.SMEM(row_counts.shape, jnp.int32),
+                dma((3,)),
                 pltpu.VMEM((2, 2, OWN, LANES), F32),
                 pltpu.VMEM((2, 2, HALO, LANES), F32),
                 pltpu.VMEM((2, WIDE, HALO, LANES), F32),
@@ -523,9 +558,9 @@
                 pltpu.VMEM((KRYLOV, half, C_ROWS, LANES), F32),
                 pltpu.VMEM((CYCLES, 1, LANES), F32),
                 pltpu.VMEM((CYCLES, n_patch, 1, LANES), F32),
-                dma((14,)), dma((14,)), dma((4,)), dma((4,)), dma((4,)), dma((4,)),
+                dma((22,)), dma((22,)), dma((4,)), dma((4,)), dma((4,)), dma((4,)),
                 dma((3, n_grp)), dma((3, n_grp)),
-                dma((CYCLES, n_patch - 1)), dma((CYCLES, n_patch - 1)),
+                dma((CYCLES,)), dma((CYCLES,)),
             ],
             compiler_params=pltpu.CompilerParams(
                 collective_id=0, has_side_effects=True, vmem_limit_bytes=40 << 20

time: 90.4 us -> 56.2 us (0.62)
  Pallas kernels: 87.2 us -> 52.9 us
    pallas_call x1, Pallas kernels: 87.2 us -> 52.9 us  [per_device(): pl.pallas_call(functools.partial(kernel, n_patch, n_grp), out_shape=jax.S...]
where the time goes in v3:
time: 56.2 us; the launch traced here: 55.9 us
  Pallas kernels  52.9 us (94%)
  local copies, waits for them, and re-layouts  2.33 us (4%)
  between operations  0.67 us (1%)
    pallas_call x1, Pallas kernels, per_device(): pl.pallas_call(functools.partial(kernel, n_patch, n_grp), out_shape=jax.S...  52.9 us
    unnamed x5, local copies, waits for them, and re-layouts  2.33 us

profile of v3, /device:TPU:1, one launch (start us, length us, event | category | flops | bytes accessed | tf_op | source)
XLA Modules:
  0.0 55.9 jit_solution(13570710548427141077)
XLA Ops:
  0.7 0.0 copy-start
  0.7 0.8 %copy-done = bf16[2,128,128]{2,1,0:T(8,128)(2,1)S(1)} copy-done((bf16[2,128,128]{2,1,0:T(8,128)(2,1)S(1)}, bf16[2,128,128]{2,1,0:T(8,128)(2,1)}, u32[]{:S(2)}) %copy-start) | copy-done | bytes 65560
  1.5 0.0 copy-start.1
  1.5 0.8 %copy-done.1 = bf16[2,128,128]{2,1,0:T(8,128)(2,1)S(1)} copy-done((bf16[2,128,128]{2,1,0:T(8,128)(2,1)S(1)}, bf16[2,128,128]{2,1,0:T(8,128)(2,1)}, u32[]{:S(2)}) %copy-start.1) | copy-done | bytes 65560
  2.3 52.9 %shard_map.37 = f32[2,128,128]{2,1,0:T(8,128)S(1)} custom-call(bf16[2,128,128]{2,1,0:T(8,128)(2,1)S(1)} %copy-done, bf16[2,128,128]{2,1,0:T(8,128)(2,1)S(1)} %copy-done.1, s32[1]{0:T(128)S(6)} %copy.5.count_hbm), custom_call_target="tpu_custom_call" | custom-call | tf_op jit(solution)/shard_map/pallas_call | solution.py:533
  55.3 0.7 %copy.6 = f32[2,128,128]{2,1,0:T(8,128)} copy(f32[2,128,128]{2,1,0:T(8,128)S(1)} %shard_map.37) | data formatting | bytes 262144
Async XLA Ops:
  0.7 0.8 %copy-start = (bf16[2,128,128]{2,1,0:T(8,128)(2,1)S(1)}, bf16[2,128,128]{2,1,0:T(8,128)(2,1)}, u32[]{:S(2)}) copy-start(bf16[2,128,128]{2,1,0:T(8,128)(2,1)} %rs_hbm.1) | copy-start | bytes 196612
  1.5 0.8 %copy-start.1 = (bf16[2,128,128]{2,1,0:T(8,128)(2,1)S(1)}, bf16[2,128,128]{2,1,0:T(8,128)(2,1)}, u32[]{:S(2)}) copy-start(bf16[2,128,128]{2,1,0:T(8,128)(2,1)} %cf_hbm.1) | copy-start | bytes 196612

commit v4 on v3

--- a/solution.py
+++ b/solution.py
@@ -57,20 +57,13 @@
     return pl.ds(offset + 8 * i, 8)
 
 
-def kernel(n_patch, n_grp, rs_hbm, cf_hbm, count_hbm, out_ref,
-           rs_ref, cf_ref, count_ref, in_sem, own, last, low, high, kf, gain, diag, cx, cy, cz, u0, u1, total, coarse, packed, gathered,
-           kc, ccx, ccy, ccz, cdiag, basis, part, parts,
+def kernel(n_patch, n_grp, own, count_ref, out_ref,
+            last, low, high, kf, gain, diag, cx, cy, cz, u0, u1, total, coarse, packed, gathered,
+           kc, ccx, ccy, ccz, cdiag, basis, images, part, parts,
            p_send, p_recv, b_send, b_recv, w_send, w_recv, c_send, c_recv, s_send, s_recv):
     half = n_grp // 2
     p = lax.axis_index("patch")
     g = lax.axis_index("grp")
-    loads = [
-        pltpu.make_async_copy(src, dst, in_sem.at[i])
-        for i, (src, dst) in enumerate(((count_hbm, count_ref), (cf_hbm, cf_ref), (rs_hbm, rs_ref)))
-    ]
-    for copy in loads:
-        copy.start()
-
     lane = lax.broadcasted_iota(jnp.int32, (8, LANES), 1)
     row = lax.broadcasted_iota(jnp.int32, (8, LANES), 0)
     even = lane % 2 == 0
@@ -81,88 +74,23 @@
 
     barrier = pltpu.get_barrier_semaphore()
     for dp in (-1, 1):
-        for dg in (-2, -1, 1, 2):
+        for dg in (0, -2, -1, 1, 2):
             peer = (lax.rem(p + dp + n_patch, n_patch), lax.rem(g + dg + n_grp, n_grp))
             pl.semaphore_signal(barrier, inc=1, device_id=peer, device_id_type=MESH)
     for dg in range(1, n_grp):
         pl.semaphore_signal(barrier, inc=1, device_id=(p, lax.rem(g + dg, n_grp)), device_id_type=MESH)
 
     def greet(i):
-        peer = (lax.rem(p + i + 1, n_patch), g)
+        peer = (lax.rem(p + i + 2, n_patch), g)
         pl.semaphore_signal(barrier, inc=1, device_id=peer, device_id_type=MESH)
 
-    loop(n_patch - 1, greet)
-    for copy in loads:
-        copy.wait()
+    loop(n_patch - 3, greet)
     count = count_ref[0]
     two = count >= 2
 
-    for a, ref in ((0, cf_ref), (1, rs_ref)):
+    for a in range(2):
         for w in range(2):
-            for half_rows in range(CAP):
-                rows = slice(PATCH * half_rows, PATCH * (half_rows + 1))
-                value = ref[w, rows, :].astype(F32)
-                if half_rows:
-                    value = jnp.where(two, value, 0.0)
-                own[a, w, rows, :] = value
-                kf[a, 4 + w, FIRST + PATCH * half_rows:FIRST + PATCH * (half_rows + 1), :] = value
             last[a, w] = jnp.where(two, own[a, w, OWN - HALO:, :], own[a, w, PATCH - HALO:PATCH, :])
-
-    guards = jnp.zeros((GUARD, LANES), F32)
-    for ref in (u0, u1, cy):
-        for w in range(WIDE):
-            ref[w, 0:GUARD, :] = guards
-            ref[w, ROWS - GUARD:, :] = guards
-    for w in range(WIDE):
-        kf[0, w, 0:GUARD, :] = guards
-        kf[0, w, ROWS - GUARD:, :] = guards
-    for j in range(half):
-        for ref in (kc, ccy):
-            ref[j, 0:GUARD, :] = guards
-            ref[j, C_ROWS - GUARD:, :] = guards
-        for m in range(KRYLOV):
-            basis[m, j, 0:GUARD, :] = guards
-            basis[m, j, C_ROWS - GUARD:, :] = guards
-
-    def clear(ref):
-        ref[...] = jnp.zeros(ref.shape, ref.dtype)
-
-    @pl.when(p == 0)
-    def _():
-        clear(low)
-
-    @pl.when(p == n_patch - 1)
-    def _():
-        clear(high)
-
-    def outside(planes):
-        for w in planes:
-            def wipe(i, w=w):
-                rows = at_tile(i, 0)
-                kf[0, w, rows, :] = zero
-                kf[1, w, rows, :] = zero
-                u1[w, rows, :] = zero
-
-            loop(ROWS // 8, wipe)
-            for a in range(2):
-                for ref in (low, high):
-                    ref[a, w] = jnp.zeros((HALO, LANES), F32)
-
-    @pl.when(g < 2)
-    def _():
-        outside((0, 1))
-
-    @pl.when(g < 1)
-    def _():
-        outside((2, 3))
-
-    @pl.when(g > n_grp - 3)
-    def _():
-        outside((8, 9))
-
-    @pl.when(g > n_grp - 2)
-    def _():
-        outside((6, 7))
 
     pl.semaphore_wait(barrier, n_patch + n_grp + 6)
 
@@ -209,6 +137,67 @@
 
     start(conduct_halo)
     start(source_halo)
+
+    for a in range(2):
+        for w in range(2):
+            kf[a, 4 + w, FIRST:FIRST + OWN, :] = own[a, w]
+
+    guards = jnp.zeros((GUARD, LANES), F32)
+    for ref in (u0, u1, cy):
+        for w in range(WIDE):
+            ref[w, 0:GUARD, :] = guards
+            ref[w, ROWS - GUARD:, :] = guards
+    for w in range(WIDE):
+        kf[0, w, 0:GUARD, :] = guards
+        kf[0, w, ROWS - GUARD:, :] = guards
+    for j in range(half):
+        for ref in (kc, ccy):
+            ref[j, 0:GUARD, :] = guards
+            ref[j, C_ROWS - GUARD:, :] = guards
+        for m in range(KRYLOV):
+            basis[m, j, 0:GUARD, :] = guards
+            basis[m, j, C_ROWS - GUARD:, :] = guards
+
+    def clear(ref):
+        ref[...] = jnp.zeros(ref.shape, ref.dtype)
+
+    @pl.when(p == 0)
+    def _():
+        clear(low)
+
+    @pl.when(p == n_patch - 1)
+    def _():
+        clear(high)
+
+    def outside(planes):
+        for w in planes:
+            def wipe(i, w=w):
+                rows = at_tile(i, 0)
+                kf[0, w, rows, :] = zero
+                kf[1, w, rows, :] = zero
+                u1[w, rows, :] = zero
+
+            loop(ROWS // 8, wipe)
+            for a in range(2):
+                for ref in (low, high):
+                    ref[a, w] = jnp.zeros((HALO, LANES), F32)
+
+    @pl.when(g < 2)
+    def _():
+        outside((0, 1))
+
+    @pl.when(g < 1)
+    def _():
+        outside((2, 3))
+
+    @pl.when(g > n_grp - 3)
+    def _():
+        outside((8, 9))
+
+    @pl.when(g > n_grp - 2)
+    def _():
+        outside((6, 7))
+
     arrive(conduct_halo)
 
     def extend(a, w):
@@ -426,7 +415,7 @@
             answer[i] = value * inverse[i]
         return answer
 
-    def correct(u, answer, slabs, tiles):
+    def spread(u, weigh, slabs, tiles, add):
         for s in slabs:
             at = g + s - 2
             valid = (at >= 0) & (at < n_grp)
@@ -434,18 +423,25 @@
             j, odd = lax.rem(at, half), at // half
 
             def body(i, s=s, valid=valid, j=j, odd=odd):
-                value = zero
-                for m in range(KRYLOV):
-                    value = value + answer[m] * basis[m, j, at_tile(i, GUARD), :]
+                value = weigh(j, at_tile(i, GUARD))
                 moved = jnp.where(odd == 0, lane_roll(value, 1), lane_roll(value, -1))
                 value = jnp.where(lane % 2 == odd, value, moved)
                 value = jnp.where(valid, value, 0.0)
                 for w in (2 * s, 2 * s + 1):
                     for a in range(2):
                         rows = pl.ds(GUARD + 16 * i + a, 8, stride=2)
-                        u[w, rows, :] = u[w, rows, :] + value
+                        u[w, rows, :] = u[w, rows, :] + value if add else value
 
             each(tiles, body)
+
+    def combined(answer):
+        def weigh(j, rows):
+            value = zero
+            for m in range(KRYLOV):
+                value = value + answer[m] * basis[m, j, rows, :]
+            return value
+
+        return weigh
 
     def to_basis(j, rows, value):
         basis[0, j, rows, :] = value
@@ -496,7 +492,7 @@
     arrive(third)
     leave(third)
     answer = coefficients(0)
-    correct(u1, answer, range(5), C_ALL)
+    spread(u1, combined(answer), range(5), C_ALL, True)
     sweep(u1, u0, range(1, 9), MOST)
 
     sweep(u0, u1, range(2, 8), MOST)
@@ -513,12 +509,29 @@
     for copy in second_out:
         copy.wait_send()
     everyone(0).wait_send()
+
+    sweep(u0, u1, range(4, 6), MINE)
+    for m in range(KRYLOV):
+        spread(u0, lambda j, rows, m=m: basis[m, j, rows, :], range(1, 4), C_MOST, False)
+
+        def image(i, m=m):
+            rows, centre, near = neighbours(u0, i, (4, 5))
+            for w in (4, 5):
+                images[m, w - 4, rows, :] = 0.2 * centre[w] + gain[w, rows, :] * near[w]
+
+        each(MINE, image)
     answer = coefficients(1)
-    correct(u0, answer, range(1, 4), C_MOST)
-    sweep(u0, u1, range(4, 6), MINE)
-    for w in range(2):
-        out_ref[w, 0:PATCH, :] = u1[4 + w, FIRST:FIRST + PATCH, :]
-        out_ref[w, PATCH:, :] = jnp.where(two, u1[4 + w, FIRST + PATCH:FIRST + OWN, :], 0.0)
+
+    def finish(i):
+        for w in range(2):
+            value = u1[4 + w, at_tile(i, FIRST), :]
+            for m in range(KRYLOV):
+                value = value + answer[m] * images[m, w, at_tile(i, FIRST), :]
+            if i >= PATCH // 8:
+                value = jnp.where(two, value, 0.0)
+            out_ref[w, at_tile(i, 0), :] = value
+
+    each(range(OWN // 8), finish)
     everyone(1).wait_send()
 
 
@@ -530,21 +543,17 @@
         fine = pltpu.VMEM((WIDE, ROWS, LANES), F32)
         level = pltpu.VMEM((half, C_ROWS, LANES), F32)
         dma = pltpu.SemaphoreType.DMA
+        used = lax.broadcasted_iota(jnp.int32, (2,) + right_side.shape, 2) < PATCH * row_counts[0]
+        own = jnp.where(used, jnp.stack([coefficient.astype(F32), right_side.astype(F32)]), 0.0)
         return pl.pallas_call(
             functools.partial(kernel, n_patch, n_grp),
             out_shape=jax.ShapeDtypeStruct(right_side.shape, F32),
             in_specs=[
-                pl.BlockSpec(memory_space=pltpu.HBM),
-                pl.BlockSpec(memory_space=pltpu.HBM),
-                pl.BlockSpec(memory_space=pltpu.HBM),
+                pl.BlockSpec(memory_space=pltpu.VMEM),
+                pl.BlockSpec(memory_space=pltpu.SMEM),
             ],
             out_specs=pl.BlockSpec(memory_space=pltpu.VMEM),
             scratch_shapes=[
-                pltpu.VMEM(right_side.shape, right_side.dtype),
-                pltpu.VMEM(coefficient.shape, coefficient.dtype),
-                pltpu.SMEM(row_counts.shape, jnp.int32),
-                dma((3,)),
-                pltpu.VMEM((2, 2, OWN, LANES), F32),
                 pltpu.VMEM((2, 2, HALO, LANES), F32),
                 pltpu.VMEM((2, WIDE, HALO, LANES), F32),
                 pltpu.VMEM((2, WIDE, HALO, LANES), F32),
@@ -556,6 +565,7 @@
                 pltpu.VMEM((3, n_grp, C_SENT, LANES), F32),
                 level, level, level, level, level,
                 pltpu.VMEM((KRYLOV, half, C_ROWS, LANES), F32),
+                pltpu.VMEM((KRYLOV, 2, ROWS, LANES), F32),
                 pltpu.VMEM((CYCLES, 1, LANES), F32),
                 pltpu.VMEM((CYCLES, n_patch, 1, LANES), F32),
                 dma((22,)), dma((22,)), dma((4,)), dma((4,)), dma((4,)), dma((4,)),
@@ -565,7 +575,7 @@
             compiler_params=pltpu.CompilerParams(
                 collective_id=0, has_side_effects=True, vmem_limit_bytes=40 << 20
             ),
-        )(right_side, coefficient, row_counts)
+        )(own, row_counts)
 
     return jax.shard_map(
         per_device,

time: 56.2 us -> 55 us (0.979)
  local copies, waits for them, and re-layouts: 2.33 us -> 0.66 us
  other arithmetic: 0 us -> 0.96 us
    unnamed x5 -> x1, local copies, waits for them, and re-layouts: 2.33 us -> 0.66 us
    select_n x0 -> x1, other arithmetic: none -> 0.96 us  [per_device(): jnp.where(used, jnp.stack([coefficient.astype(F32), right_side.astype(F32...]
where the time goes in v4:
time: 55 us; the launch traced here: 54.8 us
  Pallas kernels  52.5 us (95%)
  other arithmetic  0.96 us (2%)
  between operations  0.68 us (1%)
  local copies, waits for them, and re-layouts  0.66 us (1%)
    pallas_call x1, Pallas kernels, per_device(): pl.pallas_call(functools.partial(kernel, n_patch, n_grp), out_shape=jax.S...  52.5 us

profile of v4, /device:TPU:1, one launch (start us, length us, event | category | flops | bytes accessed | tf_op | source)
XLA Modules:
  0.0 54.8 jit_solution(10608869745015633453)
XLA Ops:
  0.7 1.0 %convert_select_fusion.own = f32[2,2,128,128]{3,2,1,0:T(8,128)S(1)} fusion(bf16[1,2,128,128]{3,2,1,0:T(8,128)(2,1)} %bitcast.3, bf16[1,2,128,128]{3,2,1,0:T(8,128)(2,1)} %bitcast.4, pred[128]{0:T(512)(128)(4,1)S(1)} %iota_compare_fusion), kind=kLoop, calls=%fused_computation | loop fusion | flops 196608 | bytes 393344 | tf_op jit(solution)/shard_map/jit(_where)/select_n | solution.py:547
  1.6 52.5 %shard_map.37 = f32[2,128,128]{2,1,0:T(8,128)S(1)} custom-call(f32[2,2,128,128]{3,2,1,0:T(8,128)S(1)} %convert_select_fusion.own, s32[1]{0:T(128)S(6)} %copy.5.count_ref), custom_call_target="tpu_custom_call" | custom-call | tf_op jit(solution)/shard_map/pallas_call | solution.py:548
  54.2 0.7 %copy.6 = f32[2,128,128]{2,1,0:T(8,128)} copy(f32[2,128,128]{2,1,0:T(8,128)S(1)} %shard_map.37) | data formatting | bytes 262144
  (1 shorter events, 0.0 us)

commit v5 on v4

--- a/solution.py
+++ b/solution.py
@@ -116,6 +116,8 @@
                 i = len(first)
                 first.append((dp, dg, remote(src, dst, p_send.at[i], p_recv.at[i], peer)))
     conduct_halo, source_halo = first[:14], first[14:]
+    near_halo = [c for c in conduct_halo if abs(c[1]) < 2]
+    far_halo = [c for c in conduct_halo if abs(c[1]) == 2]
 
     def start(copies):
         for dp, dg, copy in copies:
@@ -135,7 +137,8 @@
             def _(copy=copy):
                 copy.wait_send()
 
-    start(conduct_halo)
+    start(near_halo)
+    start(far_halo)
     start(source_halo)
 
     for a in range(2):
@@ -198,7 +201,7 @@
     def _():
         outside((6, 7))
 
-    arrive(conduct_halo)
+    arrive(near_halo)
 
     def extend(a, w):
         kf[a, w, GUARD:FIRST, :] = low[a, w]
@@ -207,7 +210,7 @@
         kf[a, w, middle, :] = jnp.where(two, kf[a, w, middle, :], upper)
         kf[a, w, FIRST + OWN:FIRST + OWN + HALO, :] = jnp.where(two, upper, 0.0)
 
-    for w in range(1, 9):
+    for w in range(2, 8):
         extend(0, w)
 
     inner = slice(GUARD + 8, GUARD + EXT - 8)
@@ -449,8 +452,11 @@
     def to_conduct(j, rows, value):
         kc[j, rows, :] = value
 
+    set_weights(range(3, 7), range(2, 7), ALL)
+    arrive(far_halo)
+    for w in (1, 8):
+        extend(0, w)
     set_diag(range(2, 8), ALL)
-    set_weights(range(3, 7), range(2, 7), ALL)
     arrive(source_halo)
     for w in range(2, 8):
         extend(1, w)

time: 55 us -> 55 us (level)
  no operation moved by 1% of the time
where the time goes in v5:
time: 55 us; the launch traced here: 54.8 us
  Pallas kernels  52.5 us (95%)
  other arithmetic  0.96 us (2%)
  between operations  0.68 us (1%)
  local copies, waits for them, and re-layouts  0.66 us (1%)
    pallas_call x1, Pallas kernels, per_device(): pl.pallas_call(functools.partial(kernel, n_patch, n_grp), out_shape=jax.S...  52.5 us

profile of v5, /device:TPU:1, one launch (start us, length us, event | category | flops | bytes accessed | tf_op | source)
XLA Modules:
  0.0 54.8 jit_solution(4846373642835608965)
XLA Ops:
  0.7 1.0 %convert_select_fusion.own = f32[2,2,128,128]{3,2,1,0:T(8,128)S(1)} fusion(bf16[1,2,128,128]{3,2,1,0:T(8,128)(2,1)} %bitcast.3, bf16[1,2,128,128]{3,2,1,0:T(8,128)(2,1)} %bitcast.4, pred[128]{0:T(512)(128)(4,1)S(1)} %iota_compare_fusion), kind=kLoop, calls=%fused_computation | loop fusion | flops 196608 | bytes 393344 | tf_op jit(solution)/shard_map/jit(_where)/select_n | solution.py:553
  1.6 52.5 %shard_map.37 = f32[2,128,128]{2,1,0:T(8,128)S(1)} custom-call(f32[2,2,128,128]{3,2,1,0:T(8,128)S(1)} %convert_select_fusion.own, s32[1]{0:T(128)S(6)} %copy.5.count_ref), custom_call_target="tpu_custom_call" | custom-call | tf_op jit(solution)/shard_map/pallas_call | solution.py:554
  54.1 0.7 %copy.6 = f32[2,128,128]{2,1,0:T(8,128)} copy(f32[2,128,128]{2,1,0:T(8,128)S(1)} %shard_map.37) | data formatting | bytes 262144
  (1 shorter events, 0.0 us)
